TPU v7x, 256 devices: a whole 4x4x8 slice. The times are simulated.
256 devices in a mesh: view: 8 (over z_lo, x), tile: 32 (over y, z_hi, core).
Axes of the slice: x: 4, y: 4, z: 8 (z_hi: 4, z_lo: 2; z = z_hi * 2 + z_lo), core: 2. Of those that a mesh axis runs over, the one named last changes fastest.
Arguments:
- estimate: float32 [16, 1024, 1024], P(None, 'tile', 'view'), may hold values from 0.5 to 2
- measured: bfloat16 [8, 16, 1024, 1024], P('view', None, 'tile'), may hold values from 0.05 to 12
- psf_z: float32 [8, 65], P('view'), may hold values from 0.05 to 1
- psf_xy: float32 [8, 2, 9], P('view'), may hold values from 0.1 to 1
- offsets: int32 [8, 2], P('view'), may hold values from -4 to 4, as said below
- coverage: int32 [8, 32], P('view', 'tile'), may hold values from 0 to 1, as said below
Outputs:
- restored: float32 [16, 1024, 1024], P(None, 'tile', 'view')
Inputs may be any that keep to these rules, and one draw needn't show every extreme that they name: offsets[v, 0] shifts view v along rows and offsets[v, 1] along columns; some view has a row offset of 4 and some view a column offset of -4. coverage[v, t] is 1 where view v images rows t * 32 to (t + 1) * 32 - 1, else 0; every tile is imaged by at least one view.
All inputs are finite; a program needn't handle non-finite values.
Results may differ from a plain program's by a relative error of at most 0.0006.
Values may be sent and summed in bfloat16 or wider, within the bound.
A program may use at most 64 MiB of HBM per device.

v0:
```python
import jax
import jax.numpy as jnp
from jax import lax
from jax.sharding import PartitionSpec as P

SHIFT = 4
ITERS = 2
EXACT_MATMUL = lax.Precision.HIGHEST


def shortened(shard):

    def short(part):
        return part.astype(jnp.bfloat16) if part.dtype == jnp.float32 else part

    return jax.tree.map(short, shard)


def padded(shard, sides, width):
    for axis, dim in sides:
        size, length = (lax.axis_size(axis), shard.shape[dim])
        up = [(i, (i + 1) % size) for i in range(size - 1)]
        down = [(j, i) for i, j in up]
        last = lax.slice_in_dim(shard, length - width, length, axis=dim)
        leading = lax.slice_in_dim(shard, 0, width, axis=dim)
        before = lax.ppermute(last, axis, up)
        after = lax.ppermute(leading, axis, down)
        shard = jnp.concatenate([before, shard, after], axis=dim)
    return shard


def band_stack(kernel, n_in, n_out, lead_offset):
    count_taps = kernel.shape[-1]
    rows_in = jnp.arange(n_in, dtype=jnp.int32)[:, None]
    rows_out = jnp.arange(n_out, dtype=jnp.int32)[None, :]
    tap_ids = jnp.arange(count_taps, dtype=jnp.int32)[:, None, None]
    selector = ((rows_in - rows_out + lead_offset)[None] == tap_ids).astype(jnp.float32)
    return jnp.tensordot(kernel, selector, axes=1, precision=EXACT_MATMUL)


def place_taps(kernel, shifts):
    count_taps = kernel.shape[-1]
    positions = jnp.arange(count_taps + 2 * SHIFT, dtype=jnp.int32)
    tap_ids = jnp.arange(count_taps, dtype=jnp.int32)
    selector = (
        positions[None, None, :] == tap_ids[None, :, None] + SHIFT + shifts[:, None, None]
    ).astype(jnp.float32)
    return jnp.einsum("vt,vtu->vu", kernel, selector, precision=EXACT_MATMUL)


def view_filters(psf_z, psf_xy, offsets, planes, row_count, block_cols):
    z_kernel = psf_z / jnp.sum(psf_z, axis=-1, keepdims=True)
    lateral_kernel = psf_xy / jnp.sum(psf_xy, axis=-1, keepdims=True)
    z_reach = (z_kernel.shape[-1] - 1) // 2
    depth_banded = band_stack(z_kernel, planes, planes, z_reach)
    y_taps = place_taps(lateral_kernel[:, 0], offsets[:, 0])
    x_taps = place_taps(lateral_kernel[:, 1], offsets[:, 1])
    margin = (y_taps.shape[-1] - 1) // 2
    forward = (
        band_stack(y_taps, row_count + 2 * margin, row_count, 0),
        band_stack(x_taps, 2 * block_cols, block_cols, 0),
    )
    backward = (
        band_stack(jnp.flip(y_taps, -1), row_count + 2 * margin, row_count, 0),
        band_stack(jnp.flip(x_taps, -1), 2 * block_cols, block_cols, 0),
    )
    return (depth_banded, forward, backward)


def cross_pass(widened_ratio, x_band, col_total, margin):
    block_cols = x_band.shape[-1]
    lead_shape = widened_ratio.shape[:-1]
    padded_cols = jnp.pad(
        widened_ratio, [(0, 0)] * (widened_ratio.ndim - 1) + [(0, block_cols - 2 * margin)]
    )
    head_blocks = padded_cols[..., :col_total].reshape(
        lead_shape + (col_total // block_cols, block_cols)
    )
    next_blocks = padded_cols[..., block_cols : block_cols + col_total].reshape(
        lead_shape + (col_total // block_cols, block_cols)
    )
    result = jnp.einsum(
        "vzynu,vuc->vzync", head_blocks, x_band[:, :block_cols], precision=EXACT_MATMUL
    )
    result = result + jnp.einsum(
        "vzynu,vuc->vzync", next_blocks, x_band[:, block_cols:], precision=EXACT_MATMUL
    )
    return result.reshape(lead_shape + (col_total,))


def lateral_rows(object_volume, banded_kernels, col_total, margin):
    widened_ratio = padded(shortened(object_volume), (("tile", 2),), margin).astype(
        object_volume.dtype
    )
    object_volume = jnp.einsum(
        "cnkw,ckr->cnrw", widened_ratio, banded_kernels[0], precision=EXACT_MATMUL
    )
    widened_ratio = jnp.pad(object_volume, ((0, 0), (0, 0), (0, 0), (margin, margin)))
    return cross_pass(widened_ratio, banded_kernels[1], col_total, margin)


def body(estimate, measured, psf_z, psf_xy, offsets, coverage):
    planes, row_count, col_count = estimate.shape
    margin = (psf_xy.shape[-1] - 1) // 2 + SHIFT
    current = estimate
    col_total = measured.shape[-1]
    block_cols = 128
    depth_banded, forward, backward = view_filters(
        psf_z, psf_xy, offsets, planes, row_count, block_cols
    )
    covered = coverage[:, 0].astype(jnp.float32)
    view_count = lax.psum(coverage[0, 0], "view").astype(jnp.float32)
    for iteration in range(ITERS):
        blurred = jnp.einsum(
            "rnl,nzf->rlzf",
            depth_banded,
            lax.all_gather(current.astype(jnp.bfloat16), "view", axis=2, tiled=True).astype(
                jnp.float32
            ),
            precision=EXACT_MATMUL,
        )
        blurred = lateral_rows(blurred, forward, col_total, margin)
        measurement_ratios = measured.astype(jnp.float32) / blurred
        updated_estimate = jnp.einsum(
            "rez,rzof->reof", depth_banded, measurement_ratios, precision=EXACT_MATMUL
        )
        updated_estimate = lateral_rows(updated_estimate, backward, col_total, margin)
        log_term = jnp.sum(covered[:, None, None, None] * jnp.log(updated_estimate), axis=0)
        log_total = lax.psum_scatter(log_term, "view", scatter_dimension=2, tiled=True)
        current = current * jnp.exp(log_total / view_count)
    return current


def solution(mesh):
    placed = (
        P(None, "tile", "view"),
        P("view", None, "tile", None),
        P("view", None),
        P("view", None, None),
        P("view", None),
        P("view", "tile"),
    )
    return jax.shard_map(
        body, mesh=mesh, in_specs=placed, out_specs=P(None, "tile", "view"), check_vma=False
    )
```

profile of v0, /device:TPU:16, one launch (start us, length us, event | category | flops | bytes accessed | tf_op | source)
XLA Modules:
  0.0 322.8 jit_solution(6538633816662928004)
XLA Ops:
  16.3 35.5 %all-gather.3.cloned.1.call-done = bf16[16,32,1024]{2,0,1:T(8,128)(2,1)} async-done(((bf16[16,32,128]{2,0,1:T(8,128)(2,1)}), bf16[16,32,1024]{2,0,1:T(8,128)(2,1)}) %all-gather.3.cloned.1.call-update) | async-done | bytes 1048592 | tf_op jit(solution)/shard_map/all_gather | solution.py:117
  56.0 6.8 %collective-permute-start.1 = (bf16[1,16,8,1024]{3,1,2,0:T(8,128)(2,1)S(1)}, bf16[1,16,8,1024]{3,1,2,0:T(8,128)(2,1)S(1)}, u32[]{:S(2)}, u32[]{:S(2)}) collective-permute-start(bf16[1,16,8,1024]{3,1,2,0:T(8,128)(2,1)S(1)} %get-tuple-element.14), channel_id=1, source_target_pairs={{1,0},{2,1},{3,2},{4,3},{5,4},{6,5},{7,6},{8,7},{9,8},{10,9},{11,1... | collective-permute-start | bytes 786440 | tf_op jit(solution)/shard_map/ppermute | solution.py:27
  66.6 2.7 collective-permute-done.1
  69.5 2.6 convolution_bitcast_fusion.3
  82.2 2.8 fusion.51
  85.9 2.7 collective-permute-start.2
  88.6 6.1 %collective-permute-start.3 = (bf16[1,16,8,1024]{3,1,2,0:T(8,128)(2,1)}, bf16[1,16,8,1024]{3,1,2,0:T(8,128)(2,1)}, u32[]{:S(2)}, u32[]{:S(2)}) collective-permute-start(bf16[1,16,8,1024]{3,1,2,0:T(8,128)(2,1)} %get-tuple-element.12), channel_id=1, source_target_pairs={{1,0},{2,1},{3,2},{4,3},{5,4},{6,5},{7,6},{8,7},{9,8},{10,9},{11,1... | collective-permute-start | bytes 786440 | tf_op jit(solution)/shard_map/ppermute | solution.py:27
  97.2 3.9 %collective-permute-done.3 = bf16[1,16,8,1024]{3,1,2,0:T(8,128)(2,1)} collective-permute-done((bf16[1,16,8,1024]{3,1,2,0:T(8,128)(2,1)}, bf16[1,16,8,1024]{3,1,2,0:T(8,128)(2,1)}, u32[]{:S(2)}, u32[]{:S(2)}) %collective-permute-start.3) | collective-permute-done | bytes 262176 | tf_op jit(solution)/shard_map/ppermute | solution.py:27
  102.2 2.6 convolution_bitcast_fusion.2
  112.6 4.1 %copy.12 = f32[16,32,1024]{2,0,1:T(8,128)} copy(f32[16,32,1024]{2,1,0:T(8,128)} %mul.37) | data formatting | bytes 4194304 | tf_op jit(solution)/shard_map/mul | solution.py:128
  116.8 12.0 %psum.7 = s32[]{:T(128)} all-reduce(s32[]{:T(128)} %bitcast.46), channel_id=1, replica_groups=mesh['view'=8,'tile'=32] {'view'}, use_global_device_ids=true, to_apply=%region_3.4 | all-reduce | flops 1 | bytes 8 | tf_op jit(solution)/shard_map/psum | solution.py:112
  129.5 34.0 %reduce-scatter.3.cloned.1.call-done = f32[16,32,128]{2,0,1:T(8,128)} async-done(((f32[16,32,1024]{2,0,1:T(8,128)}), f32[16,32,128]{2,0,1:T(8,128)}) %reduce-scatter.3.cloned.1.call-update) | async-done | bytes 262160 | tf_op jit(solution)/shard_map/reduce_scatter | solution.py:129
  165.5 38.6 %all-gather.5.cloned.1.call-done = bf16[16,32,1024]{2,0,1:T(8,128)(2,1)} async-done(((bf16[16,32,128]{2,0,1:T(8,128)(2,1)}), bf16[16,32,1024]{2,0,1:T(8,128)(2,1)}) %all-gather.5.cloned.1.call-update) | async-done | bytes 1048592 | tf_op jit(solution)/shard_map/all_gather | solution.py:117
  208.4 6.7 %collective-permute-start.5 = (bf16[1,16,8,1024]{3,1,2,0:T(8,128)(2,1)S(1)}, bf16[1,16,8,1024]{3,1,2,0:T(8,128)(2,1)S(1)}, u32[]{:S(2)}, u32[]{:S(2)}) collective-permute-start(bf16[1,16,8,1024]{3,1,2,0:T(8,128)(2,1)S(1)} %get-tuple-element.10), channel_id=1, source_target_pairs={{1,0},{2,1},{3,2},{4,3},{5,4},{6,5},{7,6},{8,7},{9,8},{10,9},{11,1... | collective-permute-start | bytes 786440 | tf_op jit(solution)/shard_map/ppermute | solution.py:27
  215.1 4.0 %collective-permute-done.4 = bf16[1,16,8,1024]{3,1,2,0:T(8,128)(2,1)S(1)} collective-permute-done((bf16[1,16,8,1024]{3,1,2,0:T(8,128)(2,1)S(1)}, bf16[1,16,8,1024]{3,1,2,0:T(8,128)(2,1)S(1)}, u32[]{:S(2)}, u32[]{:S(2)}) %collective-permute-start.4) | collective-permute-done | bytes 262176 | tf_op jit(solution)/shard_map/ppermute | solution.py:26
  219.0 2.7 collective-permute-done.5
  221.9 2.6 convolution_bitcast_fusion.1
  234.2 2.8 fusion.48
  237.1 2.7 collective-permute-start.6
  239.8 6.3 %collective-permute-start.7 = (bf16[1,16,8,1024]{3,1,2,0:T(8,128)(2,1)S(1)}, bf16[1,16,8,1024]{3,1,2,0:T(8,128)(2,1)S(1)}, u32[]{:S(2)}, u32[]{:S(2)}) collective-permute-start(bf16[1,16,8,1024]{3,1,2,0:T(8,128)(2,1)S(1)} %get-tuple-element.8), channel_id=1, source_target_pairs={{1,0},{2,1},{3,2},{4,3},{5,4},{6,5},{7,6},{8,7},{9,8},{10,9},{11,1... | collective-permute-start | bytes 786440 | tf_op jit(solution)/shard_map/ppermute | solution.py:27
  248.2 3.8 %collective-permute-done.7 = bf16[1,16,8,1024]{3,1,2,0:T(8,128)(2,1)S(1)} collective-permute-done((bf16[1,16,8,1024]{3,1,2,0:T(8,128)(2,1)S(1)}, bf16[1,16,8,1024]{3,1,2,0:T(8,128)(2,1)S(1)}, u32[]{:S(2)}, u32[]{:S(2)}) %collective-permute-start.7) | collective-permute-done | bytes 262176 | tf_op jit(solution)/shard_map/ppermute | solution.py:27
  252.2 2.6 convolution_bitcast_fusion
  263.0 4.1 %copy.18 = f32[16,32,1024]{2,0,1:T(8,128)} copy(f32[16,32,1024]{2,1,0:T(8,128)} %mul.40) | data formatting | bytes 4194304 | tf_op jit(solution)/shard_map/mul | solution.py:128
  267.2 46.9 %reduce-scatter.5.cloned.1.call-done = f32[16,32,128]{2,0,1:T(8,128)} async-done(((f32[16,32,1024]{2,0,1:T(8,128)}), f32[16,32,128]{2,0,1:T(8,128)}) %reduce-scatter.5.cloned.1.call-update) | async-done | bytes 262160 | tf_op jit(solution)/shard_map/reduce_scatter | solution.py:129
  (102 shorter events, 68.0 us)
Async XLA Ops:
  6.5 45.2 %all-gather.3.cloned.1.call-start = ((), (), s32[]{:S(2)}) async-start(), calls=%async_computation.2 | async-start | bytes 1179648 | tf_op jit(solution)/shard_map/all_gather | solution.py:117
  8.3 155.2 %reduce-scatter.3.cloned.1.call-start = ((), (), s32[]{:S(2)}) async-start(), calls=%async_computation.3 | async-start | bytes 2359296 | tf_op jit(solution)/shard_map/reduce_scatter | solution.py:129
  16.3 47.9 %copy-start.3 = (pred[17,256,128]{2,1,0:T(32,128)(4,1)}, pred[17,256,128]{2,1,0:T(32,128)(4,1)S(1)}, u32[]{:S(2)}) copy-start(pred[17,256,128]{2,1,0:T(32,128)(4,1)S(1)} %iota_compare_fusion) | copy-start | bytes 1671172
  54.0 12.6 %collective-permute-start = (bf16[1,16,8,1024]{3,1,2,0:T(8,128)(2,1)S(1)}, bf16[1,16,8,1024]{3,1,2,0:T(8,128)(2,1)S(1)}, u32[]{:S(2)}, u32[]{:S(2)}) collective-permute-start(bf16[1,16,8,1024]{3,1,2,0:T(8,128)(2,1)S(1)} %get-tuple-element.13), channel_id=1, source_target_pairs={{0,1},{1,2},{2,3},{3,4},{4,5},{5,6},{6,7},{7,8},{8,9},{9,10},{10,1... | collective-permute-start | bytes 786440 | tf_op jit(solution)/shard_map/ppermute | solution.py:26
  56.0 13.3 %collective-permute-start.1 = (bf16[1,16,8,1024]{3,1,2,0:T(8,128)(2,1)S(1)}, bf16[1,16,8,1024]{3,1,2,0:T(8,128)(2,1)S(1)}, u32[]{:S(2)}, u32[]{:S(2)}) collective-permute-start(bf16[1,16,8,1024]{3,1,2,0:T(8,128)(2,1)S(1)} %get-tuple-element.14), channel_id=1, source_target_pairs={{1,0},{2,1},{3,2},{4,3},{5,4},{6,5},{7,6},{8,7},{9,8},{10,9},{11,1... | collective-permute-start | bytes 786440 | tf_op jit(solution)/shard_map/ppermute | solution.py:27
  63.0 6.5 %copy-start.9 = (f32[48,32]{1,0:T(8,128)}, f32[48,32]{1,0:T(8,128)S(1)}, u32[]{:S(2)}) copy-start(f32[48,32]{1,0:T(8,128)S(1)} %get-tuple-element.6) | copy-start | bytes 18436
  63.0 39.2 %copy-start.7 = (f32[48,32]{1,0:T(8,128)}, f32[48,32]{1,0:T(8,128)S(1)}, u32[]{:S(2)}) copy-start(f32[48,32]{1,0:T(8,128)S(1)} %get-tuple-element.5) | copy-start | bytes 18436
  78.3 1.9 copy-start
  82.2 13.2 %copy-start.4 = (pred[17,256,128]{2,1,0:T(32,128)(4,1)S(1)}, pred[17,256,128]{2,1,0:T(32,128)(4,1)}, u32[]{:S(2)}) copy-start(pred[17,256,128]{2,1,0:T(32,128)(4,1)} %copy-done.3) | copy-start | bytes 1671172
  85.9 11.3 %collective-permute-start.2 = (bf16[1,16,8,1024]{3,1,2,0:T(8,128)(2,1)}, bf16[1,16,8,1024]{3,1,2,0:T(8,128)(2,1)S(1)}, u32[]{:S(2)}, u32[]{:S(2)}) collective-permute-start(bf16[1,16,8,1024]{3,1,2,0:T(8,128)(2,1)} %get-tuple-element.11), channel_id=1, source_target_pairs={{0,1},{1,2},{2,3},{3,4},{4,5},{5,6},{6,7},{7,8},{8,9},{9,10},{10,1... | collective-permute-start | bytes 786440 | tf_op jit(solution)/shard_map/ppermute | solution.py:26
  88.6 12.5 %collective-permute-start.3 = (bf16[1,16,8,1024]{3,1,2,0:T(8,128)(2,1)}, bf16[1,16,8,1024]{3,1,2,0:T(8,128)(2,1)}, u32[]{:S(2)}, u32[]{:S(2)}) collective-permute-start(bf16[1,16,8,1024]{3,1,2,0:T(8,128)(2,1)} %get-tuple-element.12), channel_id=1, source_target_pairs={{1,0},{2,1},{3,2},{4,3},{5,4},{6,5},{7,6},{8,7},{9,8},{10,9},{11,1... | collective-permute-start | bytes 786440 | tf_op jit(solution)/shard_map/ppermute | solution.py:27
  96.6 12.7 %copy-start.5 = (f32[1,256,128]{2,0,1:T(1,128)}, f32[1,256,128]{2,0,1:T(1,128)S(1)}, u32[]{:S(2)}) copy-start(f32[1,256,128]{2,0,1:T(1,128)S(1)} %fusion) | copy-start | bytes 393220
  116.8 46.7 %copy-start.1 = (f32[16,32,128]{2,1,0:T(8,128)S(1)}, f32[16,32,128]{2,1,0:T(8,128)}, u32[]{:S(2)}) copy-start(f32[16,32,128]{2,1,0:T(8,128)} %param.6) | copy-start | bytes 786436
  116.8 87.4 %all-gather.5.cloned.1.call-start = ((), (), s32[]{:S(2)}) async-start(), calls=%async_computation.4 | async-start | bytes 1179648 | tf_op jit(solution)/shard_map/all_gather | solution.py:117
  165.3 148.8 %reduce-scatter.5.cloned.1.call-start = ((), (), s32[]{:S(2)}) async-start(), calls=%async_computation.5 | async-start | bytes 2359296 | tf_op jit(solution)/shard_map/reduce_scatter | solution.py:129
  206.4 15.5 %copy-start.10 = (f32[48,32]{1,0:T(8,128)S(1)}, f32[48,32]{1,0:T(8,128)}, u32[]{:S(2)}) copy-start(f32[48,32]{1,0:T(8,128)} %copy-done.9) | copy-start | bytes 18436
  206.5 12.6 %collective-permute-start.4 = (bf16[1,16,8,1024]{3,1,2,0:T(8,128)(2,1)S(1)}, bf16[1,16,8,1024]{3,1,2,0:T(8,128)(2,1)S(1)}, u32[]{:S(2)}, u32[]{:S(2)}) collective-permute-start(bf16[1,16,8,1024]{3,1,2,0:T(8,128)(2,1)S(1)} %get-tuple-element.9), channel_id=1, source_target_pairs={{0,1},{1,2},{2,3},{3,4},{4,5},{5,6},{6,7},{7,8},{8,9},{9,10},{10,1... | collective-permute-start | bytes 786440 | tf_op jit(solution)/shard_map/ppermute | solution.py:26
  208.4 13.3 %collective-permute-start.5 = (bf16[1,16,8,1024]{3,1,2,0:T(8,128)(2,1)S(1)}, bf16[1,16,8,1024]{3,1,2,0:T(8,128)(2,1)S(1)}, u32[]{:S(2)}, u32[]{:S(2)}) collective-permute-start(bf16[1,16,8,1024]{3,1,2,0:T(8,128)(2,1)S(1)} %get-tuple-element.10), channel_id=1, source_target_pairs={{1,0},{2,1},{3,2},{4,3},{5,4},{6,5},{7,6},{8,7},{9,8},{10,9},{11,1... | collective-permute-start | bytes 786440 | tf_op jit(solution)/shard_map/ppermute | solution.py:27
  237.1 15.2 %copy-start.8 = (f32[48,32]{1,0:T(8,128)S(1)}, f32[48,32]{1,0:T(8,128)}, u32[]{:S(2)}) copy-start(f32[48,32]{1,0:T(8,128)} %copy-done.7) | copy-start | bytes 18436
  237.1 11.1 %collective-permute-start.6 = (bf16[1,16,8,1024]{3,1,2,0:T(8,128)(2,1)S(1)}, bf16[1,16,8,1024]{3,1,2,0:T(8,128)(2,1)S(1)}, u32[]{:S(2)}, u32[]{:S(2)}) collective-permute-start(bf16[1,16,8,1024]{3,1,2,0:T(8,128)(2,1)S(1)} %get-tuple-element.7), channel_id=1, source_target_pairs={{0,1},{1,2},{2,3},{3,4},{4,5},{5,6},{6,7},{7,8},{8,9},{9,10},{10,1... | collective-permute-start | bytes 786440 | tf_op jit(solution)/shard_map/ppermute | solution.py:26
  239.8 12.2 %collective-permute-start.7 = (bf16[1,16,8,1024]{3,1,2,0:T(8,128)(2,1)S(1)}, bf16[1,16,8,1024]{3,1,2,0:T(8,128)(2,1)S(1)}, u32[]{:S(2)}, u32[]{:S(2)}) collective-permute-start(bf16[1,16,8,1024]{3,1,2,0:T(8,128)(2,1)S(1)} %get-tuple-element.8), channel_id=1, source_target_pairs={{1,0},{2,1},{3,2},{4,3},{5,4},{6,5},{7,6},{8,7},{9,8},{10,9},{11,1... | collective-permute-start | bytes 786440 | tf_op jit(solution)/shard_map/ppermute | solution.py:27
  256.9 0.9 copy-start.6
  267.2 47.0 %copy-start.2 = (f32[16,32,128]{2,0,1:T(8,128)S(1)}, f32[16,32,128]{2,0,1:T(8,128)}, u32[]{:S(2)}) copy-start(f32[16,32,128]{2,0,1:T(8,128)} %reduce-scatter.3.cloned.1.call-done) | copy-start | bytes 786436
Sparse Core Ops, SparseCore 0:
  9.1 42.6 all-gather.2
  116.9 46.5 reduce-scatter.2
  165.4 38.6 all-gather.4
  267.3 46.7 reduce-scatter.4
where the time goes:
time: 326 us; the launch traced here: 323 us
  waiting for transfers between devices  177 us (54%)
  matrix products  39.7 us (12%)
  starting transfers between devices  35.3 us (11%)
  local copies, waits for them, and re-layouts  30.2 us (9%)
  between operations  15.2 us (5%)
  other arithmetic  13.2 us (4%)
  blocking collectives  12 us (4%)
    reduce_scatter x2, waiting for transfers between devices, body(): lax.psum_scatter(log_term, 'view', scatter_dimension=2, tiled=True)  80.9 us
    all_gather x2, waiting for transfers between devices, body(): lax.all_gather(current.astype(jnp.bfloat16), 'view', axis=2, tiled=True)  74.1 us
    ppermute x4, starting transfers between devices, padded(): after = lax.ppermute(leading, axis, down)  25.8 us
    ppermute x4, waiting for transfers between devices, padded(): after = lax.ppermute(leading, axis, down)  13.1 us
    psum x1, blocking collectives, body(): view_count = lax.psum(coverage[0, 0], 'view').astype(jnp.float32)  12 us
    mul x4, local copies, waits for them, and re-layouts, body(): covered[:, None, None, None] * jnp.log(updated_estimate)  11.3 us
    dot_general x4, matrix products, lateral_rows(): jnp.einsum('cnkw,ckr->cnrw', widened_ratio, banded_kernels[0], precision=...  10.4 us
    ppermute x4, starting transfers between devices, padded(): before = lax.ppermute(last, axis, up)  9.23 us
  transfers between devices with their start and end apart: 12, of which 12 were waited for; matrix products, arithmetic and copies ran while one was open for 3% of the time, Pallas kernels for 0%

commit v1 on v0

--- a/solution.py
+++ b/solution.py
@@ -114,9 +114,12 @@
         blurred = jnp.einsum(
             "rnl,nzf->rlzf",
             depth_banded,
-            lax.all_gather(current.astype(jnp.bfloat16), "view", axis=2, tiled=True).astype(
-                jnp.float32
-            ),
+            jnp.concatenate(
+                lax.all_to_all(
+                    jnp.stack([current.astype(jnp.bfloat16)] * lax.axis_size("view")), "view", 0, 0
+                ),
+                axis=2,
+            ).astype(jnp.float32),
             precision=EXACT_MATMUL,
         )
         blurred = lateral_rows(blurred, forward, col_total, margin)

time: 326 us -> 261 us (0.80)
  waiting for transfers between devices: 177 us -> 110 us
  blocking collectives: 12 us -> 22.9 us
  local copies, waits for them, and re-layouts: 30.2 us -> 19.8 us
  starting transfers between devices: 35.3 us -> 41.5 us
    all_gather x2 -> x0, waiting for transfers between devices: 74.1 us -> none  [body(): lax.all_gather(current.astype(jnp.bfloat16), 'view', axis=2, tiled=True)]
    all_to_all x0 -> x1, blocking collectives: none -> 14 us  [body(): lax.all_to_all(jnp.stack([current.astype(jnp.bfloat16)] * lax.axis_size('...]
    all_to_all x0 -> x1, waiting for transfers between devices: none -> 10.2 us  [body(): lax.all_to_all(jnp.stack([current.astype(jnp.bfloat16)] * lax.axis_size('...]
    mul x4 -> x2, local copies, waits for them, and re-layouts: 11.3 us -> 3.02 us  [body(): covered[:, None, None, None] * jnp.log(updated_estimate)]
    all_to_all x0 -> x1, starting transfers between devices: none -> 5.65 us  [body(): lax.all_to_all(jnp.stack([current.astype(jnp.bfloat16)] * lax.axis_size('...]
  transfers between devices with their start and end apart: 12 -> 11, of which waited for: 12 -> 10; matrix products, arithmetic and copies ran while one was open for 3% -> 3% of each run, Pallas kernels for 0% -> 0%
where the time goes in v1:
time: 261 us; the launch traced here: 258 us
  waiting for transfers between devices  110 us (42%)
  starting transfers between devices  41.5 us (16%)
  matrix products  36.7 us (14%)
  blocking collectives  22.9 us (9%)
  local copies, waits for them, and re-layouts  19.8 us (8%)
  between operations  15.5 us (6%)
  other arithmetic  11.6 us (4%)
    reduce_scatter x2, waiting for transfers between devices, body(): lax.psum_scatter(log_term, 'view', scatter_dimension=2, tiled=True)  79.9 us
    ppermute x4, starting transfers between devices, padded(): after = lax.ppermute(leading, axis, down)  25.8 us
    all_to_all x1, blocking collectives, body(): lax.all_to_all(jnp.stack([current.astype(jnp.bfloat16)] * lax.axis_size('...  14 us
    ppermute x4, waiting for transfers between devices, padded(): after = lax.ppermute(leading, axis, down)  11.6 us
    dot_general x4, matrix products, lateral_rows(): jnp.einsum('cnkw,ckr->cnrw', widened_ratio, banded_kernels[0], precision=...  10.4 us
    all_to_all x1, waiting for transfers between devices, body(): lax.all_to_all(jnp.stack([current.astype(jnp.bfloat16)] * lax.axis_size('...  10.2 us
    ppermute x4, starting transfers between devices, padded(): before = lax.ppermute(last, axis, up)  9.96 us
    psum x1, blocking collectives, body(): view_count = lax.psum(coverage[0, 0], 'view').astype(jnp.float32)  8.88 us
  transfers between devices with their start and end apart: 11, of which 10 were waited for; matrix products, arithmetic and copies ran while one was open for 3% of the time, Pallas kernels for 0%

profile of v1, /device:TPU:16, one launch (start us, length us, event | category | flops | bytes accessed | tf_op | source)
XLA Modules:
  0.0 257.8 jit_solution(13398358233672897865)
XLA Ops:
  8.7 5.7 %all-to-all-start = ((bf16[8,16,32,128]{3,1,2,0:T(8,128)(2,1)}), bf16[8,16,32,128]{3,1,2,0:T(8,128)(2,1)S(1)}, u32[]{:S(2)}, u32[]{:S(2)}) async-start(bf16[8,16,32,128]{3,1,2,0:T(8,128)(2,1)} %stack.4), calls=%async_computation | async-start | bytes 2097152 | tf_op jit(solution)/shard_map/all_to_all | solution.py:118
  19.0 10.2 %all-to-all-done = bf16[8,16,32,128]{3,1,2,0:T(8,128)(2,1)S(1)} async-done(((bf16[8,16,32,128]{3,1,2,0:T(8,128)(2,1)}), bf16[8,16,32,128]{3,1,2,0:T(8,128)(2,1)S(1)}, u32[]{:S(2)}, u32[]{:S(2)}) %all-to-all-start) | async-done | bytes 1048608 | tf_op jit(solution)/shard_map/all_to_all | solution.py:118
  32.2 7.2 %collective-permute-start.1 = (bf16[1,16,8,1024]{3,1,2,0:T(8,128)(2,1)S(1)}, bf16[1,16,8,1024]{3,1,2,0:T(8,128)(2,1)S(1)}, u32[]{:S(2)}, u32[]{:S(2)}) collective-permute-start(bf16[1,16,8,1024]{3,1,2,0:T(8,128)(2,1)S(1)} %get-tuple-element.14), channel_id=1, source_target_pairs={{1,0},{2,1},{3,2},{4,3},{5,4},{6,5},{7,6},{8,7},{9,8},{10,9},{11,1... | collective-permute-start | bytes 786440 | tf_op jit(solution)/shard_map/ppermute | solution.py:27
  41.4 4.2 %collective-permute-done.1 = bf16[1,16,8,1024]{3,1,2,0:T(8,128)(2,1)S(1)} collective-permute-done((bf16[1,16,8,1024]{3,1,2,0:T(8,128)(2,1)S(1)}, bf16[1,16,8,1024]{3,1,2,0:T(8,128)(2,1)S(1)}, u32[]{:S(2)}, u32[]{:S(2)}) %collective-permute-start.1) | collective-permute-done | bytes 262176 | tf_op jit(solution)/shard_map/ppermute | solution.py:27
  45.8 2.6 %convolution_bitcast_fusion.3 = f32[1,16,32,1024]{3,2,1,0:T(8,128)S(1)} fusion(bf16[16,48,1024]{2,0,1:T(8,128)(2,1)S(1)} %maximum_bitcast_fusion, f32[48,32]{1,0:T(8,128)S(1)} %get-tuple-element.6), kind=kOutput, calls=%fused_computation.38 | convolution fusion | flops 301989888 | bytes 3676160 | tf_op jit(solution)/shard_map/cnkw,ckr->cnrw/dot_general | solution.py:95
  58.3 2.8 %fusion.51 = bf16[1,16,32,1024]{3,1,2,0:T(8,128)(2,1)S(1)} fusion(f32[16,16,1]{1,0,2:T(8,128)S(1)} %bitcast.252, f32[16,32,1024]{2,1,0:T(8,128)S(1)} %fusion.4), kind=kOutput, calls=%fused_computation.56 | convolution fusion | flops 101187584 | bytes 3146752 | tf_op jit(solution)/shard_map/rez,rzof->reof/dot_general | solution.py:127
  61.9 3.3 %collective-permute-start.2 = (bf16[1,16,8,1024]{3,1,2,0:T(8,128)(2,1)}, bf16[1,16,8,1024]{3,1,2,0:T(8,128)(2,1)S(1)}, u32[]{:S(2)}, u32[]{:S(2)}) collective-permute-start(bf16[1,16,8,1024]{3,1,2,0:T(8,128)(2,1)} %get-tuple-element.11), channel_id=1, source_target_pairs={{0,1},{1,2},{2,3},{3,4},{4,5},{5,6},{6,7},{7,8},{8,9},{9,10},{10,1... | collective-permute-start | bytes 786440 | tf_op jit(solution)/shard_map/ppermute | solution.py:26
  65.3 5.4 %collective-permute-start.3 = (bf16[1,16,8,1024]{3,1,2,0:T(8,128)(2,1)}, bf16[1,16,8,1024]{3,1,2,0:T(8,128)(2,1)S(1)}, u32[]{:S(2)}, u32[]{:S(2)}) collective-permute-start(bf16[1,16,8,1024]{3,1,2,0:T(8,128)(2,1)} %get-tuple-element.12), channel_id=1, source_target_pairs={{1,0},{2,1},{3,2},{4,3},{5,4},{6,5},{7,6},{8,7},{9,8},{10,9},{11,1... | collective-permute-start | bytes 786440 | tf_op jit(solution)/shard_map/ppermute | solution.py:27
  72.6 2.0 collective-permute-done.2
  76.8 2.6 %convolution_bitcast_fusion.2 = f32[1,16,32,1024]{3,2,1,0:T(8,128)S(1)} fusion(bf16[16,48,1024]{2,0,1:T(8,128)(2,1)S(1)} %maximum_bitcast_fusion.1, f32[48,32]{1,0:T(8,128)S(1)} %copy-done.7), kind=kOutput, calls=%fused_computation.37 | convolution fusion | flops 301989888 | bytes 3676160 | tf_op jit(solution)/shard_map/cnkw,ckr->cnrw/dot_general | solution.py:95
  87.3 8.9 %psum.7 = s32[]{:T(128)} all-reduce(s32[]{:T(128)} %bitcast.47), channel_id=1, replica_groups=mesh['view'=8,'tile'=32] {'view'}, use_global_device_ids=true, to_apply=%region_3.4 | all-reduce | flops 1 | bytes 8 | tf_op jit(solution)/shard_map/psum | solution.py:112
  96.8 35.8 %reduce-scatter.3.cloned.1.call-done = f32[16,32,128]{2,1,0:T(8,128)} async-done(((f32[16,32,1024]{2,1,0:T(8,128)}), f32[16,32,128]{2,1,0:T(8,128)}) %reduce-scatter.3.cloned.1.call-update) | async-done | bytes 262160 | tf_op jit(solution)/shard_map/reduce_scatter | solution.py:132
  133.8 14.0 %all_to_all.10 = bf16[8,16,32,128]{3,1,2,0:T(8,128)(2,1)S(1)} all-to-all(bf16[8,16,32,128]{3,1,2,0:T(8,128)(2,1)S(1)} %stack.5), channel_id=1, replica_groups=mesh['view'=8,'tile'=32] {'view'}, dimensions={0} | all-to-all | bytes 2097152 | tf_op jit(solution)/shard_map/all_to_all | solution.py:118
  150.8 7.1 %collective-permute-start.5 = (bf16[1,16,8,1024]{3,1,2,0:T(8,128)(2,1)S(1)}, bf16[1,16,8,1024]{3,1,2,0:T(8,128)(2,1)S(1)}, u32[]{:S(2)}, u32[]{:S(2)}) collective-permute-start(bf16[1,16,8,1024]{3,1,2,0:T(8,128)(2,1)S(1)} %get-tuple-element.10), channel_id=1, source_target_pairs={{1,0},{2,1},{3,2},{4,3},{5,4},{6,5},{7,6},{8,7},{9,8},{10,9},{11,1... | collective-permute-start | bytes 786440 | tf_op jit(solution)/shard_map/ppermute | solution.py:27
  157.8 4.3 %collective-permute-done.4 = bf16[1,16,8,1024]{3,1,2,0:T(8,128)(2,1)S(1)} collective-permute-done((bf16[1,16,8,1024]{3,1,2,0:T(8,128)(2,1)S(1)}, bf16[1,16,8,1024]{3,1,2,0:T(8,128)(2,1)S(1)}, u32[]{:S(2)}, u32[]{:S(2)}) %collective-permute-start.4) | collective-permute-done | bytes 262176 | tf_op jit(solution)/shard_map/ppermute | solution.py:26
  162.1 2.0 collective-permute-done.5
  164.3 2.6 %convolution_bitcast_fusion.1 = f32[1,16,32,1024]{3,2,1,0:T(8,128)S(1)} fusion(bf16[16,48,1024]{2,0,1:T(8,128)(2,1)S(1)} %maximum_bitcast_fusion.2, f32[48,32]{1,0:T(8,128)S(1)} %copy-done.10), kind=kOutput, calls=%fused_computation.36 | convolution fusion | flops 301989888 | bytes 3676160 | tf_op jit(solution)/shard_map/cnkw,ckr->cnrw/dot_general | solution.py:95
  176.6 2.8 %fusion.48 = bf16[1,16,32,1024]{3,1,2,0:T(8,128)(2,1)S(1)} fusion(f32[16,16,1]{1,0,2:T(8,128)S(1)} %bitcast.254, f32[16,32,1024]{2,1,0:T(8,128)S(1)} %fusion.5), kind=kOutput, calls=%fused_computation.55 | convolution fusion | flops 101187584 | bytes 3146752 | tf_op jit(solution)/shard_map/rez,rzof->reof/dot_general | solution.py:127
  179.5 2.8 %collective-permute-start.6 = (bf16[1,16,8,1024]{3,1,2,0:T(8,128)(2,1)S(1)}, bf16[1,16,8,1024]{3,1,2,0:T(8,128)(2,1)S(1)}, u32[]{:S(2)}, u32[]{:S(2)}) collective-permute-start(bf16[1,16,8,1024]{3,1,2,0:T(8,128)(2,1)S(1)} %get-tuple-element.7), channel_id=1, source_target_pairs={{0,1},{1,2},{2,3},{3,4},{4,5},{5,6},{6,7},{7,8},{8,9},{9,10},{10,1... | collective-permute-start | bytes 786440 | tf_op jit(solution)/shard_map/ppermute | solution.py:26
  182.3 6.1 %collective-permute-start.7 = (bf16[1,16,8,1024]{3,1,2,0:T(8,128)(2,1)S(1)}, bf16[1,16,8,1024]{3,1,2,0:T(8,128)(2,1)S(1)}, u32[]{:S(2)}, u32[]{:S(2)}) collective-permute-start(bf16[1,16,8,1024]{3,1,2,0:T(8,128)(2,1)S(1)} %get-tuple-element.8), channel_id=1, source_target_pairs={{1,0},{2,1},{3,2},{4,3},{5,4},{6,5},{7,6},{8,7},{9,8},{10,9},{11,1... | collective-permute-start | bytes 786440 | tf_op jit(solution)/shard_map/ppermute | solution.py:27
  188.4 2.0 collective-permute-done.6
  190.4 3.5 %collective-permute-done.7 = bf16[1,16,8,1024]{3,1,2,0:T(8,128)(2,1)S(1)} collective-permute-done((bf16[1,16,8,1024]{3,1,2,0:T(8,128)(2,1)S(1)}, bf16[1,16,8,1024]{3,1,2,0:T(8,128)(2,1)S(1)}, u32[]{:S(2)}, u32[]{:S(2)}) %collective-permute-start.7) | collective-permute-done | bytes 262176 | tf_op jit(solution)/shard_map/ppermute | solution.py:27
  194.1 2.6 %convolution_bitcast_fusion = f32[1,16,32,1024]{3,2,1,0:T(8,128)S(1)} fusion(bf16[16,48,1024]{2,0,1:T(8,128)(2,1)S(1)} %maximum_bitcast_fusion.3, f32[48,32]{1,0:T(8,128)S(1)} %copy-done.8), kind=kOutput, calls=%fused_computation.35 | convolution fusion | flops 301989888 | bytes 3676160 | tf_op jit(solution)/shard_map/cnkw,ckr->cnrw/dot_general | solution.py:95
  204.9 44.1 %reduce-scatter.5.cloned.1.call-done = f32[16,32,128]{2,1,0:T(8,128)} async-done(((f32[16,32,1024]{2,1,0:T(8,128)}), f32[16,32,128]{2,1,0:T(8,128)}) %reduce-scatter.5.cloned.1.call-update) | async-done | bytes 262160 | tf_op jit(solution)/shard_map/reduce_scatter | solution.py:132
  (106 shorter events, 57.9 us)
Async XLA Ops:
  6.5 7.9 %copy-start.12 = (s32[1,2]{1,0:T(1,128)S(1)}, s32[1,2]{1,0:T(1,128)}, u32[]{:S(2)}) copy-start(s32[1,2]{1,0:T(1,128)} %param.10) | copy-start | bytes 28
  6.5 8.5 %copy-start.13 = (f32[1,65]{1,0:T(1,128)S(1)}, f32[1,65]{1,0:T(1,128)}, u32[]{:S(2)}) copy-start(f32[1,65]{1,0:T(1,128)} %param.8) | copy-start | bytes 784
  6.5 9.1 %copy-start.11 = (f32[1,2,9]{2,1,0:T(2,128)S(1)}, f32[1,2,9]{2,1,0:T(2,128)}, u32[]{:S(2)}) copy-start(f32[1,2,9]{2,1,0:T(2,128)} %param.9) | copy-start | bytes 220
  8.7 20.5 %all-to-all-start = ((bf16[8,16,32,128]{3,1,2,0:T(8,128)(2,1)}), bf16[8,16,32,128]{3,1,2,0:T(8,128)(2,1)S(1)}, u32[]{:S(2)}, u32[]{:S(2)}) async-start(bf16[8,16,32,128]{3,1,2,0:T(8,128)(2,1)} %stack.4), calls=%async_computation | async-start | bytes 2097152 | tf_op jit(solution)/shard_map/all_to_all | solution.py:118
  14.4 118.2 %reduce-scatter.3.cloned.1.call-start = ((), (), s32[]{:S(2)}) async-start(), calls=%async_computation.4 | async-start | bytes 2359296 | tf_op jit(solution)/shard_map/reduce_scatter | solution.py:132
  19.0 22.4 %copy-start.3 = (pred[17,256,128]{2,1,0:T(32,128)(4,1)}, pred[17,256,128]{2,1,0:T(32,128)(4,1)S(1)}, u32[]{:S(2)}) copy-start(pred[17,256,128]{2,1,0:T(32,128)(4,1)S(1)} %iota_compare_fusion) | copy-start | bytes 1671172
  30.3 11.1 %collective-permute-start = (bf16[1,16,8,1024]{3,1,2,0:T(8,128)(2,1)S(1)}, bf16[1,16,8,1024]{3,1,2,0:T(8,128)(2,1)S(1)}, u32[]{:S(2)}, u32[]{:S(2)}) collective-permute-start(bf16[1,16,8,1024]{3,1,2,0:T(8,128)(2,1)S(1)} %get-tuple-element.13), channel_id=1, source_target_pairs={{0,1},{1,2},{2,3},{3,4},{4,5},{5,6},{6,7},{7,8},{8,9},{9,10},{10,1... | collective-permute-start | bytes 786440 | tf_op jit(solution)/shard_map/ppermute | solution.py:26
  32.2 13.4 %collective-permute-start.1 = (bf16[1,16,8,1024]{3,1,2,0:T(8,128)(2,1)S(1)}, bf16[1,16,8,1024]{3,1,2,0:T(8,128)(2,1)S(1)}, u32[]{:S(2)}, u32[]{:S(2)}) collective-permute-start(bf16[1,16,8,1024]{3,1,2,0:T(8,128)(2,1)S(1)} %get-tuple-element.14), channel_id=1, source_target_pairs={{1,0},{2,1},{3,2},{4,3},{5,4},{6,5},{7,6},{8,7},{9,8},{10,9},{11,1... | collective-permute-start | bytes 786440 | tf_op jit(solution)/shard_map/ppermute | solution.py:27
  40.1 5.6 %copy-start.9 = (f32[48,32]{1,0:T(8,128)}, f32[48,32]{1,0:T(8,128)S(1)}, u32[]{:S(2)}) copy-start(f32[48,32]{1,0:T(8,128)S(1)} %get-tuple-element.6) | copy-start | bytes 18436
  54.6 1.7 copy-start
  58.2 13.2 %copy-start.4 = (pred[17,256,128]{2,1,0:T(32,128)(4,1)S(1)}, pred[17,256,128]{2,1,0:T(32,128)(4,1)}, u32[]{:S(2)}) copy-start(pred[17,256,128]{2,1,0:T(32,128)(4,1)} %copy-done.3) | copy-start | bytes 1671172
  61.9 12.7 %collective-permute-start.2 = (bf16[1,16,8,1024]{3,1,2,0:T(8,128)(2,1)}, bf16[1,16,8,1024]{3,1,2,0:T(8,128)(2,1)S(1)}, u32[]{:S(2)}, u32[]{:S(2)}) collective-permute-start(bf16[1,16,8,1024]{3,1,2,0:T(8,128)(2,1)} %get-tuple-element.11), channel_id=1, source_target_pairs={{0,1},{1,2},{2,3},{3,4},{4,5},{5,6},{6,7},{7,8},{8,9},{9,10},{10,1... | collective-permute-start | bytes 786440 | tf_op jit(solution)/shard_map/ppermute | solution.py:26
  65.3 11.3 %collective-permute-start.3 = (bf16[1,16,8,1024]{3,1,2,0:T(8,128)(2,1)}, bf16[1,16,8,1024]{3,1,2,0:T(8,128)(2,1)S(1)}, u32[]{:S(2)}, u32[]{:S(2)}) collective-permute-start(bf16[1,16,8,1024]{3,1,2,0:T(8,128)(2,1)} %get-tuple-element.12), channel_id=1, source_target_pairs={{1,0},{2,1},{3,2},{4,3},{5,4},{6,5},{7,6},{8,7},{9,8},{10,9},{11,1... | collective-permute-start | bytes 786440 | tf_op jit(solution)/shard_map/ppermute | solution.py:27
  72.6 11.2 %copy-start.5 = (f32[1,256,128]{2,0,1:T(1,128)}, f32[1,256,128]{2,0,1:T(1,128)S(1)}, u32[]{:S(2)}) copy-start(f32[1,256,128]{2,0,1:T(1,128)S(1)} %fusion) | copy-start | bytes 393220
  72.6 4.2 %copy-start.7 = (f32[48,32]{1,0:T(8,128)S(1)}, f32[48,32]{1,0:T(8,128)}, u32[]{:S(2)}) copy-start(f32[48,32]{1,0:T(8,128)} %get-tuple-element.5) | copy-start | bytes 18436
  87.2 45.4 %copy-start.1 = (f32[16,32,128]{2,1,0:T(8,128)S(1)}, f32[16,32,128]{2,1,0:T(8,128)}, u32[]{:S(2)}) copy-start(f32[16,32,128]{2,1,0:T(8,128)} %param.6) | copy-start | bytes 786436
  87.2 161.8 %reduce-scatter.5.cloned.1.call-start = ((), (), s32[]{:S(2)}) async-start(), calls=%async_computation.5 | async-start | bytes 2359296 | tf_op jit(solution)/shard_map/reduce_scatter | solution.py:132
  148.8 15.5 %copy-start.10 = (f32[48,32]{1,0:T(8,128)S(1)}, f32[48,32]{1,0:T(8,128)}, u32[]{:S(2)}) copy-start(f32[48,32]{1,0:T(8,128)} %copy-done.9) | copy-start | bytes 18436
  148.9 13.3 %collective-permute-start.4 = (bf16[1,16,8,1024]{3,1,2,0:T(8,128)(2,1)S(1)}, bf16[1,16,8,1024]{3,1,2,0:T(8,128)(2,1)S(1)}, u32[]{:S(2)}, u32[]{:S(2)}) collective-permute-start(bf16[1,16,8,1024]{3,1,2,0:T(8,128)(2,1)S(1)} %get-tuple-element.9), channel_id=1, source_target_pairs={{0,1},{1,2},{2,3},{3,4},{4,5},{5,6},{6,7},{7,8},{8,9},{9,10},{10,1... | collective-permute-start | bytes 786440 | tf_op jit(solution)/shard_map/ppermute | solution.py:26
  150.8 13.3 %collective-permute-start.5 = (bf16[1,16,8,1024]{3,1,2,0:T(8,128)(2,1)S(1)}, bf16[1,16,8,1024]{3,1,2,0:T(8,128)(2,1)S(1)}, u32[]{:S(2)}, u32[]{:S(2)}) collective-permute-start(bf16[1,16,8,1024]{3,1,2,0:T(8,128)(2,1)S(1)} %get-tuple-element.10), channel_id=1, source_target_pairs={{1,0},{2,1},{3,2},{4,3},{5,4},{6,5},{7,6},{8,7},{9,8},{10,9},{11,1... | collective-permute-start | bytes 786440 | tf_op jit(solution)/shard_map/ppermute | solution.py:27
  179.5 14.6 %copy-start.8 = (f32[48,32]{1,0:T(8,128)S(1)}, f32[48,32]{1,0:T(8,128)}, u32[]{:S(2)}) copy-start(f32[48,32]{1,0:T(8,128)} %get-tuple-element.5) | copy-start | bytes 18436
  179.5 10.9 %collective-permute-start.6 = (bf16[1,16,8,1024]{3,1,2,0:T(8,128)(2,1)S(1)}, bf16[1,16,8,1024]{3,1,2,0:T(8,128)(2,1)S(1)}, u32[]{:S(2)}, u32[]{:S(2)}) collective-permute-start(bf16[1,16,8,1024]{3,1,2,0:T(8,128)(2,1)S(1)} %get-tuple-element.7), channel_id=1, source_target_pairs={{0,1},{1,2},{2,3},{3,4},{4,5},{5,6},{6,7},{7,8},{8,9},{9,10},{10,1... | collective-permute-start | bytes 786440 | tf_op jit(solution)/shard_map/ppermute | solution.py:26
  182.3 11.6 %collective-permute-start.7 = (bf16[1,16,8,1024]{3,1,2,0:T(8,128)(2,1)S(1)}, bf16[1,16,8,1024]{3,1,2,0:T(8,128)(2,1)S(1)}, u32[]{:S(2)}, u32[]{:S(2)}) collective-permute-start(bf16[1,16,8,1024]{3,1,2,0:T(8,128)(2,1)S(1)} %get-tuple-element.8), channel_id=1, source_target_pairs={{1,0},{2,1},{3,2},{4,3},{5,4},{6,5},{7,6},{8,7},{9,8},{10,9},{11,1... | collective-permute-start | bytes 786440 | tf_op jit(solution)/shard_map/ppermute | solution.py:27
  204.9 44.2 %copy-start.2 = (f32[16,32,128]{2,1,0:T(8,128)S(1)}, f32[16,32,128]{2,1,0:T(8,128)}, u32[]{:S(2)}) copy-start(f32[16,32,128]{2,1,0:T(8,128)} %reduce-scatter.3.cloned.1.call-done) | copy-start | bytes 786436
  (1 other events, 0.9 us)
Sparse Core Ops, SparseCore 0:
  87.4 45.1 reduce-scatter.2
  205.1 43.9 reduce-scatter.4
